TPU v7x, 512 devices: a whole 4x8x8 slice. The times are simulated.
512 devices in a mesh: gz: 128 (over y, z, core), gy: 4 (over x).
Axes of the slice: x: 4, y: 8, z: 8, core: 2. Of those that a mesh axis runs over, the one named last changes fastest.
Arguments:
- image: bfloat16 [128, 512, 512], P('gz', 'gy'), may hold values from -30 to 30, as said below
- conv_one: bfloat16 [16, 9], replicated, may hold values from -2 to 2
- conv_two: bfloat16 [32, 144], replicated, may hold values from -0.5 to 0.5
- tissue: int32 [128, 4096], P('gz', 'gy'), may hold values 0 or 1
Outputs:
- increments: float32 [2, 128, 4096], P(None, 'gz', 'gy')
Inputs may be any that keep to these rules, and one draw needn't show every extreme that they name: `image`: pixel intensities of each section's crop.
All inputs are finite; a program needn't handle non-finite values. No bound on the sum of `tissue` on one device may be relied on, other than what follows from the above.
Results may differ from a plain program's by a relative error of at most 0.0029.
Values may be sent and summed in bfloat16 or wider, within the bound.
A program may use at most 64 MiB of HBM per device.

v0:
```python
import jax
import jax.numpy as jnp
from jax import lax
from jax.experimental import pallas as pl
from jax.experimental.pallas import tpu as pltpu
from jax.sharding import PartitionSpec as P

BF, F32 = jnp.bfloat16, jnp.float32
MESH = pl.DeviceIdType.MESH
GROUP = 16
SPRING, ANCHOR = 8.0, 0.02
ROWS = 32
SCALE = 32 ** (-0.5) * 1.4426950408889634


def iota(shape, dim):
    return lax.broadcasted_iota(jnp.int32, shape, dim)


def mm(left, right):
    return jnp.dot(left, right, preferred_element_type=F32)


def half_turn(x):
    return pltpu.roll(x, 64, 1)


def inv_sym(a, b, c):
    r = 1.0 / (a * c - b * b)
    return c * r, -b * r, a * r


def mul22(l, r):
    return (
        l[0] * r[0] + l[1] * r[2],
        l[0] * r[1] + l[1] * r[3],
        l[2] * r[0] + l[3] * r[2],
        l[2] * r[1] + l[3] * r[3],
    )


def mul21(l, v):
    return l[0] * v[0] + l[1] * v[1], l[2] * v[0] + l[3] * v[1]


def full(sym):
    return sym[0], sym[1], sym[1], sym[2]


def build_weights(w1_ref, w2_ref, sel, w1b, w2p):
    for part in range(4):
        base = iota((128, 128), 0) + 128 * part - 4 * iota((128, 128), 1)
        for v in range(7):
            sel[128 * part : 128 * part + 128, 128 * v : 128 * v + 128] = jnp.where(
                base == v - 3, 1.0, 0.0
            ).astype(BF)
    tap, col = iota((9, 256), 0), iota((9, 256), 1)
    a = (tap * 11) >> 5
    da = (col & 31) - 15 - a
    db = (col >> 5) - (tap - 3 * a)
    w1 = w1_ref[...]
    base = jnp.concatenate(
        [mm(w1, jnp.where((da == 0) & (db == 2 * b), 1.0, 0.0).astype(BF)) for b in range(3)], axis=0
    )
    for f in range(8):
        moved = base if f == 0 else pltpu.roll(base, 2 * f, 1)
        w1b[48 * f : 48 * f + 48, :] = moved[:, :224].astype(BF)
    k, n = iota((144, 144), 0), iota((144, 144), 1)
    ab = n >> 4
    perm = jnp.where(k == 9 * (n & 15) + ab, 1.0, 0.0).astype(BF)
    w2p[...] = mm(w2_ref[...], perm).astype(BF)


def split_columns(window, rows, sel, xs):
    for pair in range(4):
        width = 256 if pair < 3 else 128
        out = mm(window[...], sel[:, 256 * pair : 256 * pair + width]).astype(BF)
        xs[2 * pair, 16 : 16 + rows, :] = out[:, :128]
        if pair < 3:
            xs[2 * pair + 1, 16 : 16 + rows, :] = out[:, 128:]


def conv_rows(xs, w1b, fm, half, low):
    def column(block):
        start = pl.multiple_of(16 * block, 16)
        return jnp.concatenate([xs[v, pl.ds(start, 32), :] for v in range(7)], axis=0)

    right = jnp.concatenate([column(low), column(low + half)], axis=1)
    out = jnp.maximum(mm(w1b[...], right), 0.0).astype(BF)
    fm[pl.ds(pl.multiple_of(384 * low, 128), 384), :] = out[:, :128]
    fm[pl.ds(pl.multiple_of(384 * (low + half), 128), 384), :] = out[:, 128:]


def conv_features(fm, w2p, first, count):
    right = jnp.concatenate(
        [fm[pl.ds(pl.multiple_of(96 * (first + q) - 48, 16), 144), :] for q in range(count)], axis=1
    )
    return jnp.maximum(mm(w2p[...], right), 0.0).astype(BF).astype(F32)


def own_pair(fm, w2p, rall, p):
    feats = conv_features(fm, w2p, 4 + 2 * p, 2)
    chunk = (iota((32, 256), 1) & 127) >> 4
    rall[p] = jnp.concatenate(
        [jnp.where(chunk == m, feats, 0.0) for m in range(8)], axis=0
    ).astype(BF)


def next_group(fm, w2p, lall, row_base, g):
    feats = conv_features(fm, w2p, 4 * g + 2, 4)
    stack = jnp.concatenate(
        [
            feats[:, 128 * q : 128 * q + 128] * (row_base + 4 * g + q < 128).astype(F32)
            for q in range(4)
        ],
        axis=0,
    )
    turned = pltpu.roll(stack, 6, 1).T
    inside = iota((128, 128), 0) >= 6
    body = jnp.where(inside, turned, 0.0)
    tail = jnp.where(inside[:16], 0.0, turned[:16])
    ext = jnp.concatenate([body, tail], axis=0)
    rot = [ext] + [pltpu.roll(ext, 32 * k, 1) for k in range(1, 4)]
    lane = iota((32, 128), 1) >> 5
    for q in range(4):
        halves = []
        for h in range(2):
            pick = [rot[(g4 - q) % 4][64 * h + 16 * g4 : 64 * h + 16 * g4 + 32] for g4 in range(4)]
            halves.append(
                jnp.where(
                    lane < 2,
                    jnp.where(lane == 0, pick[0], pick[1]),
                    jnp.where(lane == 2, pick[2], pick[3]),
                )
            )
        lall[pl.ds(pl.multiple_of(128 * g + 32 * q, 32), 32), :] = jnp.concatenate(
            halves, axis=1
        ).astype(BF)


def correlate_pair(lall, rall, scores, mom, p):
    scores[...] = mm(lall[pl.ds(pl.multiple_of(64 * p, 64), 14 * ROWS), :], rall[p])
    shift = iota((ROWS, 128), 0) - (iota((ROWS, 128), 1) & 15)
    valid = (shift >= 0) & (shift <= 12)
    b = (shift - 6).astype(F32)
    for par in range(2):
        cols = slice(128 * par, 128 * par + 128)

        def at(n):
            return scores[ROWS * (n + par) : ROWS * (n + par) + ROWS, cols]

        high = at(0)
        for n in range(1, 13):
            high = jnp.maximum(high, at(n))
        top = jnp.max(jnp.where(valid, high, -3e38), axis=0, keepdims=True)
        t0 = t1 = t2 = None
        for n in range(12, -1, -1):
            e = jnp.exp2((at(n) - top) * SCALE)
            t0 = e if t0 is None else t0 + e
            t1 = t0 if t1 is None else t1 + t0
            t2 = t1 if t2 is None else t2 + t1
        t0 = jnp.where(valid, t0, 0.0)
        t1 = jnp.where(valid, t1, 0.0)
        t2 = jnp.where(valid, t2, 0.0)
        tb = t0 * b
        for field, term in enumerate((t0, t1, t2, tb, tb * b, t1 * b)):
            mom[p, field : field + 1, cols] = jnp.sum(term, axis=0, keepdims=True)


def node_blocks(mom, marks_ref, last, send):
    m0, m1, m2, mb, mbb, mab = (mom[:, f, :] for f in range(6))
    r = 1.0 / m0
    n1, mean_b = m1 * r, mb * r
    mean_a = n1 - 7.0
    var_a = (2.0 * m2 - 15.0 * m1) * r + 49.0 - mean_a * mean_a + 1.0
    var_b = mbb * r - mean_b * mean_b + 1.0
    cov = mab * r - n1 * mean_b
    i_aa, i_ab, i_bb = inv_sym(var_a, cov, var_b)
    p_a = i_aa * mean_a + i_ab * mean_b
    p_b = i_ab * mean_a + i_bb * mean_b
    stack = jnp.concatenate([x[:, :128] + x[:, 128:] for x in (i_aa, i_ab, i_bb, p_a, p_b)], axis=0)
    pool = jnp.where((iota((128, 128), 0) >> 1) == (iota((128, 128), 1) & 63), 0.25, 0.0)
    pooled = jnp.dot(stack, pool, precision=lax.Precision.HIGHEST, preferred_element_type=F32)
    spread = jnp.where((iota((16, 8), 0) >> 1) == iota((16, 8), 1), 1.0, 0.0)
    marks = mm(spread, marks_ref[...].astype(F32))
    same = (iota((16, 128), 0) & 1) == (iota((16, 128), 1) >> 6)
    marks = jnp.where(same, marks, half_turn(marks)) * jnp.where(last, 0.0, 1.0)
    for f in range(5):
        data = pooled[16 * f : 16 * f + 16] * marks
        for q in range(16):
            send[q, f : f + 1, :] = data[q : q + 1]


def segment(recv, group, sections, low, high):
    left = iota((1, 128), 1) < 64
    first = None
    for j in range(GROUP):
        a, b, c, ra, rb = (
            jnp.where(left, recv[j, f : f + 1, :], recv[GROUP - 1 - j, f : f + 1, :]) for f in range(5)
        )
        section = GROUP * group + jnp.where(left, j, GROUP - 1 - j)
        ends = (section == 0) | (section == sections - 1)
        extra = jnp.where(ends, SPRING + ANCHOR, 2 * SPRING + ANCHOR)
        a, c = a + extra, c + extra
        if j == 0:
            d, y = (a, b, c), (ra, rb)
            eight, none = jnp.full((1, 128), SPRING), jnp.zeros((1, 128))
            cc = (eight, none, none, eight)
        else:
            inv = tuple(SPRING * x for x in inv_sym(*d))
            iy = mul21(full(inv), y)
            d = (a - SPRING * inv[0], b - SPRING * inv[1], c - SPRING * inv[2])
            y = (ra + iy[0], rb + iy[1])
            cc = mul22(full(inv), cc)
        rows = d + y + cc
        if j < 8:
            for f, x in enumerate(rows):
                low[f, j : j + 1, :] = x
            for f, x in enumerate((a, b, c, ra, rb)):
                low[9 + f, j : j + 1, :] = x
        else:
            for f, x in enumerate(rows):
                high[f, GROUP - 1 - j : GROUP - j, :] = x
    return rows


def link_step(front, back, pk, pv):
    d, y, c = front[:3], front[3:5], front[5:]
    bd, by, bc = back[:3], back[3:5], back[5:]
    ea, eb, ec, ed = (
        bd[0] - SPRING * pk[0],
        bd[1] - SPRING * pk[1],
        bd[1] - SPRING * pk[2],
        bd[2] - SPRING * pk[3],
    )
    r = 1.0 / (ea * ed - eb * ec)
    einv = (ed * r, -eb * r, -ec * r, ea * r)
    dinv = full(inv_sym(*d))
    through = mul22(c, pk)
    lead = mul22(through, einv)
    gain = mul22(lead, bc)
    gain = (gain[0] + SPRING, gain[1], gain[2], gain[3] + SPRING)
    load = mul21(lead, (by[0] + SPRING * pv[0], by[1] + SPRING * pv[1]))
    held = mul21(c, pv)
    return mul22(dinv, gain), mul21(dinv, (y[0] + held[0] + load[0], y[1] + held[1] + load[1]))


def links(recv, group, groups, own):
    left = iota((1, 128), 1) < 64
    none = jnp.zeros((1, 128))
    pk, pv = (none,) * 4, (none,) * 2
    limit = jnp.where(left, group, groups - 1 - group)
    for j in range(groups - 1):
        here = [recv[j, f : f + 1, :] for f in range(9)]
        there = [recv[groups - 1 - j, f : f + 1, :] for f in range(9)]
        front = tuple(jnp.where(left, x, z) for x, z in zip(here, there))
        back = tuple(half_turn(jnp.where(left, z, x)) for x, z in zip(here, there))
        nk, nv = link_step(front, back, pk, pv)
        use = limit > j
        pk = tuple(jnp.where(use, n, o) for n, o in zip(nk, pk))
        pv = tuple(jnp.where(use, n, o) for n, o in zip(nv, pv))
    nk, nv = link_step(own, tuple(half_turn(x) for x in own), pk, pv)
    rk, rv = tuple(half_turn(x) for x in pk), tuple(half_turn(x) for x in pv)
    t = mul22(nk, rk)
    a, b, c, d = 1.0 - t[0], -t[1], -t[2], 1.0 - t[3]
    r = 1.0 / (a * d - b * c)
    rhs = mul21(nk, rv)
    w = mul21((d * r, -b * r, -c * r, a * r), (rhs[0] + nv[0], rhs[1] + nv[1]))
    x = mul21(rk, w)
    return half_turn(x[0] + rv[0]), half_turn(x[1] + rv[1])


def interior(low, high, bound):
    lo = [low[f] for f in range(14)]
    hi = [high[f] for f in range(9)]
    other = [half_turn(x) for x in hi[:5]]
    d = [lo[f] + other[f] - lo[9 + f] for f in range(5)]
    near = mul21(lo[5:9], bound)
    far = mul21(hi[5:9], bound)
    rhs = [d[3 + n] + near[n] + half_turn(far[n]) for n in range(2)]
    return mul21(full(inv_sym(*d[:3])), rhs)


def kernel(
    sections,
    strips,
    image,
    w1_ref,
    w2_ref,
    marks_ref,
    out_ref,
    nwin,
    owin,
    sel,
    w1b,
    w2p,
    nxs,
    oxs,
    nfm,
    ofm,
    lall,
    rall,
    scores,
    mom,
    send_a,
    recv_a,
    low,
    high,
    send_b,
    recv_b,
    send_c,
    recv_c,
    local_sem,
    isend,
    irecv,
    asend,
    arecv,
    bsend,
    brecv,
    csend,
    crecv,
):
    s, r = lax.axis_index("gz"), lax.axis_index("gy")
    groups = sections // GROUP
    group, k = lax.div(s, GROUP), lax.rem(s, GROUP)
    after, before = lax.rem(s + 1, sections), lax.rem(s + sections - 1, sections)
    down, up = lax.rem(r + 1, strips), lax.rem(r + strips - 1, strips)
    mates = [GROUP * group + lax.rem(k + o, GROUP) for o in range(GROUP)]
    peers = [GROUP * lax.rem(group + o, groups) + k for o in range(groups)]

    local = pltpu.make_async_copy(image, owin.at[pl.ds(16, 128)], local_sem)
    local.start()
    barrier = pltpu.get_barrier_semaphore()
    partners = [
        (before, r),
        (after, r),
        (before, up),
        (after, down),
        (before, down),
        (after, up),
        (s, down),
        (s, up),
    ]
    partners += [(m, r) for m in mates[1:]] + [(m, r) for m in peers[1:]]
    for place in partners:
        pl.semaphore_signal(barrier, inc=1, device_id=place, device_id_type=MESH)

    build_weights(w1_ref, w2_ref, sel, w1b, w2p)
    nxs[:, 0:16, :] = jnp.zeros((7, 16, 128), BF)
    oxs[:, 0:16, :] = jnp.zeros((7, 16, 128), BF)
    oxs[:, 160:176, :] = jnp.zeros((7, 16, 128), BF)

    pl.semaphore_wait(barrier, len(partners))

    def remote(src, dst, ssem, rsem, place):
        return pltpu.make_async_remote_copy(
            src_ref=src,
            dst_ref=dst,
            send_sem=ssem,
            recv_sem=rsem,
            device_id=place,
            device_id_type=MESH,
        )

    halo = remote(image.at[pl.ds(112, 16)], owin.at[pl.ds(0, 16)], isend.at[0], irecv.at[0], (s, down))
    moves = [
        remote(image, nwin.at[pl.ds(32, 128)], isend.at[1], irecv.at[1], (before, r)),
        remote(
            image.at[pl.ds(96, 32)], nwin.at[pl.ds(0, 32)], isend.at[2], irecv.at[2], (before, down)
        ),
        remote(
            image.at[pl.ds(0, 32)], nwin.at[pl.ds(160, 32)], isend.at[3], irecv.at[3], (before, up)
        ),
    ]
    halo.start()
    for move in moves:
        move.start()
    local.wait()
    halo.wait()

    @pl.when(r == 0)
    def _():
        owin[0:16, :] = jnp.zeros((16, 512), BF)

    split_columns(owin, 144, sel, oxs)

    def loop(count, step):
        def run(i, carry):
            step(i)
            return carry

        lax.fori_loop(0, count, run, 0)

    loop(5, lambda i: conv_rows(oxs, w1b, ofm, 5, i))
    loop(16, lambda i: own_pair(ofm, w2p, rall, i))

    for move in moves:
        move.wait()

    @pl.when(r == 0)
    def _():
        nwin[0:32, :] = jnp.zeros((32, 512), BF)

    @pl.when(r == strips - 1)
    def _():
        nwin[160:192, :] = jnp.zeros((32, 512), BF)

    split_columns(nwin, 192, sel, nxs)
    loop(6, lambda i: conv_rows(nxs, w1b, nfm, 6, i))
    loop(11, lambda i: next_group(nfm, w2p, lall, 32 * r - 6, i))
    loop(16, lambda i: correlate_pair(lall, rall, scores, mom, i))

    node_blocks(mom, marks_ref, s == sections - 1, send_a)
    moves_a = [
        remote(send_a.at[mates[o]  - GROUP * group], recv_a.at[k], asend.at[o - 1], arecv.at[o - 1], (mates[o], r))
        for o in range(1, GROUP)
    ]
    for move in moves_a:
        move.start()
    recv_a[k] = send_a[k]
    for move in moves_a:
        move.wait()

    ends = segment(recv_a, group, sections, low, high)
    for f, x in enumerate(ends):
        send_b[f : f + 1, :] = x
    moves_b = [
        remote(send_b, recv_b.at[group], bsend.at[o - 1], brecv.at[o - 1], (peers[o], r))
        for o in range(1, groups)
    ]
    for move in moves_b:
        move.start()
    recv_b[group] = send_b[...]
    for move in moves_b:
        move.wait()

    bound = links(recv_b, group, groups, ends)
    xa, xb = interior(low, high, bound)
    left8 = iota((8, 128), 1) < 64
    front = jnp.where(left8, xa, half_turn(xb))
    rear = jnp.where(left8, half_turn(xa), xb)
    for j in range(8):
        send_c[j] = front[j : j + 1]
        send_c[GROUP - 1 - j] = rear[j : j + 1]
    slot = 8 * lax.rem(k, 2) + lax.div(k, 2)
    moves_c = [
        remote(send_c.at[mates[o] - GROUP * group], recv_c.at[slot], csend.at[o - 1], crecv.at[o - 1], (mates[o], r))
        for o in range(1, GROUP)
    ]
    for move in moves_c:
        move.start()
    recv_c[slot] = send_c[k]
    for move in moves_c:
        move.wait()
    even = jnp.concatenate([recv_c[q] for q in range(8)], axis=0)
    odd = jnp.concatenate([recv_c[q] for q in range(8, 16)], axis=0)
    out_ref[0] = jnp.where(left8, even, half_turn(odd))
    out_ref[1] = jnp.where(left8, half_turn(even), odd)


def body(sections, strips, image, conv_one, conv_two, tissue):
    groups = sections // GROUP
    vmem = pl.BlockSpec(memory_space=pltpu.VMEM)
    dma = pltpu.SemaphoreType.DMA
    out = pl.pallas_call(
        lambda *refs: kernel(sections, strips, *refs),
        out_shape=jax.ShapeDtypeStruct((2, 8, 128), F32),
        in_specs=[pl.BlockSpec(memory_space=pl.ANY), vmem, vmem, vmem],
        out_specs=vmem,
        scratch_shapes=[
            pltpu.VMEM((192, 512), BF),
            pltpu.VMEM((144, 512), BF),
            pltpu.VMEM((512, 896), BF),
            pltpu.VMEM((384, 224), BF),
            pltpu.VMEM((32, 144), BF),
            pltpu.VMEM((7, 208, 128), BF),
            pltpu.VMEM((7, 176, 128), BF),
            pltpu.VMEM((12 * 384, 128), BF),
            pltpu.VMEM((10 * 384, 128), BF),
            pltpu.VMEM((44 * ROWS, 256), BF),
            pltpu.VMEM((16, 256, 256), BF),
            pltpu.VMEM((14 * ROWS, 256), F32),
            pltpu.VMEM((16, 8, 256), F32),
            pltpu.VMEM((GROUP, 5, 128), F32),
            pltpu.VMEM((GROUP, 5, 128), F32),
            pltpu.VMEM((14, 8, 128), F32),
            pltpu.VMEM((9, 8, 128), F32),
            pltpu.VMEM((9, 128), F32),
            pltpu.VMEM((groups, 9, 128), F32),
            pltpu.VMEM((GROUP, 1, 128), F32),
            pltpu.VMEM((GROUP, 1, 128), F32),
            dma,
            dma((4,)),
            dma((4,)),
            dma((GROUP - 1,)),
            dma((GROUP - 1,)),
            dma((groups - 1,)),
            dma((groups - 1,)),
            dma((GROUP - 1,)),
            dma((GROUP - 1,)),
        ],
        compiler_params=pltpu.CompilerParams(
            collective_id=0, has_side_effects=True, vmem_limit_bytes=32 * 1024 * 1024
        ),
    )(image.reshape(128, 512), conv_one, conv_two, tissue.reshape(8, 128))
    return out.reshape(2, 1, 1024)


def solution(mesh):
    sections, strips = mesh.shape["gz"], mesh.shape["gy"]
    placed = (P("gz", "gy", None), P(), P(), P("gz", "gy"))
    return jax.shard_map(
        lambda *args: body(sections, strips, *args),
        mesh=mesh,
        in_specs=placed,
        out_specs=P(None, "gz", "gy"),
        check_vma=False,
    )
```

profile of v0, /device:TPU:1, one launch (start us, length us, event | category | flops | bytes accessed | tf_op | source)
XLA Modules:
  0.0 53.5 jit_solution(6993918943918041319)
XLA Ops:
  0.0 0.0 copy-start
  0.0 0.9 %copy-done = bf16[1,128,512]{2,1,0:T(8,128)(2,1)S(1)} copy-done((bf16[1,128,512]{2,1,0:T(8,128)(2,1)S(1)}, bf16[1,128,512]{2,1,0:T(8,128)(2,1)}, u32[]{:S(2)}) %copy-start) | copy-done | bytes 131096
  0.9 0.0 copy-start.1
  0.9 0.7 %copy-done.1 = bf16[32,144]{1,0:T(8,128)(2,1)S(1)} copy-done((bf16[32,144]{1,0:T(8,128)(2,1)S(1)}, bf16[32,144]{1,0:T(8,128)(2,1)}, u32[]{:S(2)}) %copy-start.1) | copy-done | bytes 9240
  1.6 0.0 copy-start.2
  1.6 0.7 %copy-done.2 = bf16[16,9]{1,0:T(8,128)(2,1)S(1)} copy-done((bf16[16,9]{1,0:T(8,128)(2,1)S(1)}, bf16[16,9]{1,0:T(8,128)(2,1)}, u32[]{:S(2)}) %copy-start.2) | copy-done | bytes 312
  2.3 0.0 copy-start.3
  2.3 0.7 %copy-done.3 = s32[1,1024]{1,0:T(1,128)S(1)} copy-done((s32[1,1024]{1,0:T(1,128)S(1)}, s32[1,1024]{1,0:T(1,128)}, u32[]{:S(2)}) %copy-start.3) | copy-done | bytes 4120
  3.0 49.9 %shard_map.46 = f32[2,8,128]{2,1,0:T(8,128)S(1)} custom-call(bf16[128,512]{1,0:T(8,128)(2,1)S(1)} %bitcast.3, bf16[16,9]{1,0:T(8,128)(2,1)S(1)} %copy-done.2, bf16[32,144]{1,0:T(8,128)(2,1)S(1)} %copy-done.1, s32[8,128]{1,0:T(8,128)S(1)} %bitcast.5), custom_call_target="tpu_custom_call" | custom-call | tf_op jit(solution)/shard_map/pallas_call | solution.py:465
  52.9 0.6 %copy.7 = f32[2,1,1024]{2,1,0:T(1,128)} copy(f32[2,1,1024]{2,1,0:T(1,128)S(1)} %bitcast.4) | data formatting | bytes 16384
Async XLA Ops:
  0.0 0.9 %copy-start = (bf16[1,128,512]{2,1,0:T(8,128)(2,1)S(1)}, bf16[1,128,512]{2,1,0:T(8,128)(2,1)}, u32[]{:S(2)}) copy-start(bf16[1,128,512]{2,1,0:T(8,128)(2,1)} %param.4) | copy-start | bytes 393220
  0.9 0.7 %copy-start.1 = (bf16[32,144]{1,0:T(8,128)(2,1)S(1)}, bf16[32,144]{1,0:T(8,128)(2,1)}, u32[]{:S(2)}) copy-start(bf16[32,144]{1,0:T(8,128)(2,1)} %refs_2_.1) | copy-start | bytes 27652
  1.6 0.7 %copy-start.2 = (bf16[16,9]{1,0:T(8,128)(2,1)S(1)}, bf16[16,9]{1,0:T(8,128)(2,1)}, u32[]{:S(2)}) copy-start(bf16[16,9]{1,0:T(8,128)(2,1)} %refs_1_.1) | copy-start | bytes 868
  2.3 0.7 %copy-start.3 = (s32[1,1024]{1,0:T(1,128)S(1)}, s32[1,1024]{1,0:T(1,128)}, u32[]{:S(2)}) copy-start(s32[1,1024]{1,0:T(1,128)} %param.7) | copy-start | bytes 12292
where the time goes:
time: 53.8 us; the launch traced here: 53.5 us
  Pallas kernels  49.9 us (93%)
  local copies, waits for them, and re-layouts  3.59 us (7%)
    pallas_call x1, Pallas kernels, body(): pl.pallas_call(lambda *refs: kernel(sections, strips, *refs), out_shape=j...  49.9 us
    unnamed x9, local copies, waits for them, and re-layouts  3.59 us

commit v1 on v0

--- a/solution.py
+++ b/solution.py
@@ -9,6 +9,8 @@
 MESH = pl.DeviceIdType.MESH
 GROUP = 16
 SPRING, ANCHOR = 8.0, 0.02
+PARTS = 2
+VMEM_LIMIT = 60 * 1024 * 1024
 ROWS = 32
 SCALE = 32 ** (-0.5) * 1.4426950408889634
 
@@ -19,6 +21,10 @@
 
 def mm(left, right):
     return jnp.dot(left, right, preferred_element_type=F32)
+
+
+def far_first(count):
+    return sorted(range(1, count), key=lambda o: -min(o, count - o))
 
 
 def half_turn(x):
@@ -48,12 +54,8 @@
 
 
 def build_weights(w1_ref, w2_ref, sel, w1b, w2p):
-    for part in range(4):
-        base = iota((128, 128), 0) + 128 * part - 4 * iota((128, 128), 1)
-        for v in range(7):
-            sel[128 * part : 128 * part + 128, 128 * v : 128 * v + 128] = jnp.where(
-                base == v - 3, 1.0, 0.0
-            ).astype(BF)
+    col = iota((256, 256), 1)
+    sel[...] = jnp.where(iota((256, 256), 0) == 4 * (col & 63) + (col >> 6), 1.0, 0.0).astype(BF)
     tap, col = iota((9, 256), 0), iota((9, 256), 1)
     a = (tap * 11) >> 5
     da = (col & 31) - 15 - a
@@ -71,30 +73,38 @@
     w2p[...] = mm(w2_ref[...], perm).astype(BF)
 
 
-def split_columns(window, rows, sel, xs):
-    for pair in range(4):
-        width = 256 if pair < 3 else 128
-        out = mm(window[...], sel[:, 256 * pair : 256 * pair + width]).astype(BF)
-        xs[2 * pair, 16 : 16 + rows, :] = out[:, :128]
-        if pair < 3:
-            xs[2 * pair + 1, 16 : 16 + rows, :] = out[:, 128:]
+def split_columns(window, low, rows, sel, xs):
+    span = slice(16 + low, 16 + low + rows)
+    out = [mm(window[low : low + rows, 256 * h : 256 * h + 256], sel[...]) for h in range(2)]
+    lane = iota((rows, 128), 1)
+    for n in range(2):
+        one, two = (x[:, 128 * n : 128 * n + 128] for x in out)
+        even = jnp.where(lane < 64, one, half_turn(two))
+        odd = jnp.where(lane < 64, half_turn(one), two)
+        for phase, x in ((2 * n, even), (2 * n + 1, odd)):
+            xs[phase + 3, span, :] = x.astype(BF)
+            if phase > 0:
+                xs[phase - 1, span, :] = jnp.where(lane == 0, 0.0, pltpu.roll(x, 1, 1)).astype(BF)
 
 
 def conv_rows(xs, w1b, fm, half, low):
     def column(block):
-        start = pl.multiple_of(16 * block, 16)
+        start = 16 * block if isinstance(block, int) else pl.multiple_of(16 * block, 16)
         return jnp.concatenate([xs[v, pl.ds(start, 32), :] for v in range(7)], axis=0)
 
     right = jnp.concatenate([column(low), column(low + half)], axis=1)
     out = jnp.maximum(mm(w1b[...], right), 0.0).astype(BF)
-    fm[pl.ds(pl.multiple_of(384 * low, 128), 384), :] = out[:, :128]
-    fm[pl.ds(pl.multiple_of(384 * (low + half), 128), 384), :] = out[:, 128:]
+    for n in range(2):
+        start = 384 * (low + n * half)
+        start = start if isinstance(low, int) else pl.multiple_of(start, 128)
+        fm[pl.ds(start, 384), :] = out[:, 128 * n : 128 * n + 128]
 
 
 def conv_features(fm, w2p, first, count):
-    right = jnp.concatenate(
-        [fm[pl.ds(pl.multiple_of(96 * (first + q) - 48, 16), 144), :] for q in range(count)], axis=1
-    )
+    starts = [96 * (first + q) - 48 for q in range(count)]
+    if not isinstance(first, int):
+        starts = [pl.multiple_of(x, 16) for x in starts]
+    right = jnp.concatenate([fm[pl.ds(x, 144), :] for x in starts], axis=1)
     return jnp.maximum(mm(w2p[...], right), 0.0).astype(BF).astype(F32)
 
 
@@ -115,12 +125,11 @@
         ],
         axis=0,
     )
-    turned = pltpu.roll(stack, 6, 1).T
-    inside = iota((128, 128), 0) >= 6
-    body = jnp.where(inside, turned, 0.0)
-    tail = jnp.where(inside[:16], 0.0, turned[:16])
-    ext = jnp.concatenate([body, tail], axis=0)
-    rot = [ext] + [pltpu.roll(ext, 32 * k, 1) for k in range(1, 4)]
+    stack = stack.astype(BF)
+    spun = jnp.concatenate([stack] + [jnp.concatenate([stack[128 - 32 * k :], stack[: 128 - 32 * k]], axis=0) for k in range(1, 4)], axis=0)
+    place = jnp.where(iota((144, 128), 0) == iota((144, 128), 1) + 6, 1.0, 0.0).astype(BF)
+    turned = lax.dot_general(place, spun, (((1,), (1,)), ((), ())), preferred_element_type=F32)
+    rot = [turned[:, 128 * k : 128 * k + 128] for k in range(4)]
     lane = iota((32, 128), 1) >> 5
     for q in range(4):
         halves = []
@@ -133,13 +142,18 @@
                     jnp.where(lane == 2, pick[2], pick[3]),
                 )
             )
-        lall[pl.ds(pl.multiple_of(128 * g + 32 * q, 32), 32), :] = jnp.concatenate(
+        lall[128 * g + 32 * q : 128 * g + 32 * q + 32, :] = jnp.concatenate(
             halves, axis=1
         ).astype(BF)
 
 
-def correlate_pair(lall, rall, scores, mom, p):
-    scores[...] = mm(lall[pl.ds(pl.multiple_of(64 * p, 64), 14 * ROWS), :], rall[p])
+def score_part(lall, rall, scores, p, part, parts):
+    rows = 14 * ROWS // parts
+    left = lall[pl.ds(pl.multiple_of(64 * p + rows * part, 16), rows), :]
+    scores[rows * part : rows * part + rows, :] = mm(left, rall[p])
+
+
+def moments_pair(scores, mom, p, between):
     shift = iota((ROWS, 128), 0) - (iota((ROWS, 128), 1) & 15)
     valid = (shift >= 0) & (shift <= 12)
     b = (shift - 6).astype(F32)
@@ -149,10 +163,12 @@
         def at(n):
             return scores[ROWS * (n + par) : ROWS * (n + par) + ROWS, cols]
 
+        between(2 * par)
         high = at(0)
         for n in range(1, 13):
             high = jnp.maximum(high, at(n))
         top = jnp.max(jnp.where(valid, high, -3e38), axis=0, keepdims=True)
+        between(2 * par + 1)
         t0 = t1 = t2 = None
         for n in range(12, -1, -1):
             e = jnp.exp2((at(n) - top) * SCALE)
@@ -285,10 +301,13 @@
     sections,
     strips,
     image,
+    w1_hbm,
+    w2_hbm,
+    marks_hbm,
+    out_ref,
     w1_ref,
     w2_ref,
     marks_ref,
-    out_ref,
     nwin,
     owin,
     sel,
@@ -300,7 +319,8 @@
     ofm,
     lall,
     rall,
-    scores,
+    scores_a,
+    scores_b,
     mom,
     send_a,
     recv_a,
@@ -328,7 +348,13 @@
     mates = [GROUP * group + lax.rem(k + o, GROUP) for o in range(GROUP)]
     peers = [GROUP * lax.rem(group + o, groups) + k for o in range(groups)]
 
-    local = pltpu.make_async_copy(image, owin.at[pl.ds(16, 128)], local_sem)
+    local = pltpu.make_async_copy(image, owin.at[pl.ds(16, 128)], local_sem.at[0])
+    smalls = [
+        pltpu.make_async_copy(src, dst, local_sem.at[n + 1])
+        for n, (src, dst) in enumerate(((w1_hbm, w1_ref), (w2_hbm, w2_ref), (marks_hbm, marks_ref)))
+    ]
+    for move in smalls:
+        move.start()
     local.start()
     barrier = pltpu.get_barrier_semaphore()
     partners = [
@@ -345,6 +371,8 @@
     for place in partners:
         pl.semaphore_signal(barrier, inc=1, device_id=place, device_id_type=MESH)
 
+    for move in smalls:
+        move.wait()
     build_weights(w1_ref, w2_ref, sel, w1b, w2p)
     nxs[:, 0:16, :] = jnp.zeros((7, 16, 128), BF)
     oxs[:, 0:16, :] = jnp.zeros((7, 16, 128), BF)
@@ -363,76 +391,97 @@
         )
 
     halo = remote(image.at[pl.ds(112, 16)], owin.at[pl.ds(0, 16)], isend.at[0], irecv.at[0], (s, down))
-    moves = [
-        remote(image, nwin.at[pl.ds(32, 128)], isend.at[1], irecv.at[1], (before, r)),
-        remote(
-            image.at[pl.ds(96, 32)], nwin.at[pl.ds(0, 32)], isend.at[2], irecv.at[2], (before, down)
-        ),
-        remote(
-            image.at[pl.ds(0, 32)], nwin.at[pl.ds(160, 32)], isend.at[3], irecv.at[3], (before, up)
-        ),
-    ]
+    def piece(row, target, n, place):
+        return remote(
+            image.at[pl.ds(row, 32)], nwin.at[pl.ds(target, 32)], isend.at[n], irecv.at[n], place
+        )
+
+    moves = [piece(96, 0, 1, (before, down))]
+    moves += [piece(32 * c, 32 + 32 * c, 2 + c, (before, r)) for c in range(4)]
+    moves += [piece(0, 160, 6, (before, up))]
     halo.start()
-    for move in moves:
+    for move in (moves[0], moves[5], *moves[1:5]):
         move.start()
     local.wait()
-    halo.wait()
+
+    def loop(low, high, step):
+        def run(i, carry):
+            step(i)
+            return carry
+
+        lax.fori_loop(low, high, run, 0)
+
+    split_columns(owin, 16, 128, sel, oxs)
+    loop(2, 5, lambda i: conv_rows(oxs, w1b, ofm, 3, i))
+    conv_rows(oxs, w1b, ofm, 1, 8)
+    loop(3, 16, lambda i: own_pair(ofm, w2p, rall, i))
+    halo.wait_recv()
 
     @pl.when(r == 0)
     def _():
         owin[0:16, :] = jnp.zeros((16, 512), BF)
 
-    split_columns(owin, 144, sel, oxs)
-
-    def loop(count, step):
-        def run(i, carry):
-            step(i)
-            return carry
-
-        lax.fori_loop(0, count, run, 0)
-
-    loop(5, lambda i: conv_rows(oxs, w1b, ofm, 5, i))
-    loop(16, lambda i: own_pair(ofm, w2p, rall, i))
-
-    for move in moves:
-        move.wait()
-
-    @pl.when(r == 0)
-    def _():
-        nwin[0:32, :] = jnp.zeros((32, 512), BF)
-
-    @pl.when(r == strips - 1)
-    def _():
-        nwin[160:192, :] = jnp.zeros((32, 512), BF)
-
-    split_columns(nwin, 192, sel, nxs)
-    loop(6, lambda i: conv_rows(nxs, w1b, nfm, 6, i))
-    loop(11, lambda i: next_group(nfm, w2p, lall, 32 * r - 6, i))
-    loop(16, lambda i: correlate_pair(lall, rall, scores, mom, i))
+    split_columns(owin, 0, 16, sel, oxs)
+    conv_rows(oxs, w1b, ofm, 1, 0)
+    for p in range(3):
+        own_pair(ofm, w2p, rall, p)
+
+    for half in range(2):
+        for c in range(3):
+            moves[3 * half + c].wait_recv()
+        edge = 160 * half
+
+        @pl.when(r == (strips - 1) * half)
+        def _():
+            nwin[edge : edge + 32, :] = jnp.zeros((32, 512), BF)
+
+        split_columns(nwin, 96 * half, 96, sel, nxs)
+        block = 6 * half
+        conv_rows(nxs, w1b, nfm, 1, block)
+        conv_rows(nxs, w1b, nfm, 1, block + 2)
+        for g in (0,) if half == 0 else (5, 6):
+            next_group(nfm, w2p, lall, 32 * r - 6, g)
+        conv_rows(nxs, w1b, nfm, 1, block + 4)
+        for g in range(1, 5) if half == 0 else range(7, 11):
+            next_group(nfm, w2p, lall, 32 * r - 6, g)
+
+    score_part(lall, rall, scores_a, 0, 0, 1)
+
+    def two_pairs(i):
+        for now, later, p in ((scores_a, scores_b, 2 * i), (scores_b, scores_a, 2 * i + 1)):
+            q = jnp.minimum(p + 1, 15)
+
+            def ahead(n):
+                if n % (4 // PARTS) == 0:
+                    score_part(lall, rall, later, q, n // (4 // PARTS), PARTS)
+
+            moments_pair(now, mom, p, ahead)
+
+    loop(0, 8, two_pairs)
 
     node_blocks(mom, marks_ref, s == sections - 1, send_a)
     moves_a = [
         remote(send_a.at[mates[o]  - GROUP * group], recv_a.at[k], asend.at[o - 1], arecv.at[o - 1], (mates[o], r))
-        for o in range(1, GROUP)
+        for o in far_first(GROUP)
     ]
     for move in moves_a:
         move.start()
     recv_a[k] = send_a[k]
     for move in moves_a:
-        move.wait()
+        move.wait_recv()
 
     ends = segment(recv_a, group, sections, low, high)
     for f, x in enumerate(ends):
         send_b[f : f + 1, :] = x
     moves_b = [
         remote(send_b, recv_b.at[group], bsend.at[o - 1], brecv.at[o - 1], (peers[o], r))
-        for o in range(1, groups)
+        for o in far_first(groups)
     ]
     for move in moves_b:
         move.start()
     recv_b[group] = send_b[...]
     for move in moves_b:
-        move.wait()
+        move.wait_recv()
 
     bound = links(recv_b, group, groups, ends)
     xa, xb = interior(low, high, bound)
@@ -445,17 +494,19 @@
     slot = 8 * lax.rem(k, 2) + lax.div(k, 2)
     moves_c = [
         remote(send_c.at[mates[o] - GROUP * group], recv_c.at[slot], csend.at[o - 1], crecv.at[o - 1], (mates[o], r))
-        for o in range(1, GROUP)
+        for o in far_first(GROUP)
     ]
     for move in moves_c:
         move.start()
     recv_c[slot] = send_c[k]
     for move in moves_c:
-        move.wait()
+        move.wait_recv()
     even = jnp.concatenate([recv_c[q] for q in range(8)], axis=0)
     odd = jnp.concatenate([recv_c[q] for q in range(8, 16)], axis=0)
     out_ref[0] = jnp.where(left8, even, half_turn(odd))
     out_ref[1] = jnp.where(left8, half_turn(even), odd)
+    for move in (halo, *moves, *moves_a, *moves_b, *moves_c):
+        move.wait_send()
 
 
 def body(sections, strips, image, conv_one, conv_two, tissue):
@@ -465,12 +516,15 @@
     out = pl.pallas_call(
         lambda *refs: kernel(sections, strips, *refs),
         out_shape=jax.ShapeDtypeStruct((2, 8, 128), F32),
-        in_specs=[pl.BlockSpec(memory_space=pl.ANY), vmem, vmem, vmem],
+        in_specs=[pl.BlockSpec(memory_space=pl.ANY)] * 4,
         out_specs=vmem,
         scratch_shapes=[
+            pltpu.VMEM((16, 9), BF),
+            pltpu.VMEM((32, 144), BF),
+            pltpu.VMEM((8, 128), jnp.int32),
             pltpu.VMEM((192, 512), BF),
             pltpu.VMEM((144, 512), BF),
-            pltpu.VMEM((512, 896), BF),
+            pltpu.VMEM((256, 256), BF),
             pltpu.VMEM((384, 224), BF),
             pltpu.VMEM((32, 144), BF),
             pltpu.VMEM((7, 208, 128), BF),
@@ -479,6 +533,7 @@
             pltpu.VMEM((10 * 384, 128), BF),
             pltpu.VMEM((44 * ROWS, 256), BF),
             pltpu.VMEM((16, 256, 256), BF),
+            pltpu.VMEM((14 * ROWS, 256), F32),
             pltpu.VMEM((14 * ROWS, 256), F32),
             pltpu.VMEM((16, 8, 256), F32),
             pltpu.VMEM((GROUP, 5, 128), F32),
@@ -489,9 +544,9 @@
             pltpu.VMEM((groups, 9, 128), F32),
             pltpu.VMEM((GROUP, 1, 128), F32),
             pltpu.VMEM((GROUP, 1, 128), F32),
-            dma,
             dma((4,)),
-            dma((4,)),
+            dma((7,)),
+            dma((7,)),
             dma((GROUP - 1,)),
             dma((GROUP - 1,)),
             dma((groups - 1,)),
@@ -500,7 +555,7 @@
             dma((GROUP - 1,)),
         ],
         compiler_params=pltpu.CompilerParams(
-            collective_id=0, has_side_effects=True, vmem_limit_bytes=32 * 1024 * 1024
+            collective_id=0, has_side_effects=True, vmem_limit_bytes=VMEM_LIMIT
         ),
     )(image.reshape(128, 512), conv_one, conv_two, tissue.reshape(8, 128))
     return out.reshape(2, 1, 1024)

time: 53.8 us -> 44.9 us (0.83)
  Pallas kernels: 49.9 us -> 43.4 us
  local copies, waits for them, and re-layouts: 3.59 us -> 1.3 us
    pallas_call x1, Pallas kernels: 49.9 us -> 43.4 us  [body(): pl.pallas_call(lambda *refs: kernel(sections, strips, *refs), out_shape=j...]
    unnamed x9 -> x1, local copies, waits for them, and re-layouts: 3.59 us -> 1.3 us
where the time goes in v1:
time: 44.9 us; the launch traced here: 44.7 us
  Pallas kernels  43.4 us (97%)
  local copies, waits for them, and re-layouts  1.3 us (3%)
    pallas_call x1, Pallas kernels, body(): pl.pallas_call(lambda *refs: kernel(sections, strips, *refs), out_shape=j...  43.4 us
    unnamed x1, local copies, waits for them, and re-layouts  1.3 us

profile of v1, /device:TPU:1, one launch (start us, length us, event | category | flops | bytes accessed | tf_op | source)
XLA Modules:
  0.0 44.7 jit_solution(1879898002767618032)
XLA Ops:
  0.0 43.4 %shard_map.46 = f32[2,8,128]{2,1,0:T(8,128)} custom-call(bf16[128,512]{1,0:T(8,128)(2,1)} %bitcast.3, bf16[16,9]{1,0:T(8,128)(2,1)} %refs_1_.1, bf16[32,144]{1,0:T(8,128)(2,1)} %refs_2_.1, s32[8,128]{1,0:T(8,128)} %bitcast.5), custom_call_target="tpu_custom_call" | custom-call | tf_op jit(solution)/shard_map/pallas_call | solution.py:516
  43.4 1.3 %copy.7 = f32[2,1,1024]{2,1,0:T(1,128)} copy(f32[2,1,1024]{2,1,0:T(1,128)} %bitcast.4) | data formatting | bytes 16384

commit v2 on v1

--- a/solution.py
+++ b/solution.py
@@ -9,7 +9,7 @@
 MESH = pl.DeviceIdType.MESH
 GROUP = 16
 SPRING, ANCHOR = 8.0, 0.02
-PARTS = 2
+AHEAD, BUFFERS = 3, 4
 VMEM_LIMIT = 60 * 1024 * 1024
 ROWS = 32
 SCALE = 32 ** (-0.5) * 1.4426950408889634
@@ -126,10 +126,9 @@
         axis=0,
     )
     stack = stack.astype(BF)
-    spun = jnp.concatenate([stack] + [jnp.concatenate([stack[128 - 32 * k :], stack[: 128 - 32 * k]], axis=0) for k in range(1, 4)], axis=0)
     place = jnp.where(iota((144, 128), 0) == iota((144, 128), 1) + 6, 1.0, 0.0).astype(BF)
-    turned = lax.dot_general(place, spun, (((1,), (1,)), ((), ())), preferred_element_type=F32)
-    rot = [turned[:, 128 * k : 128 * k + 128] for k in range(4)]
+    ext = lax.dot_general(place, stack, (((1,), (1,)), ((), ())), preferred_element_type=F32)
+    rot = [ext] + [pltpu.roll(ext, 32 * k, 1) for k in range(1, 4)]
     lane = iota((32, 128), 1) >> 5
     for q in range(4):
         halves = []
@@ -147,13 +146,11 @@
         ).astype(BF)
 
 
-def score_part(lall, rall, scores, p, part, parts):
-    rows = 14 * ROWS // parts
-    left = lall[pl.ds(pl.multiple_of(64 * p + rows * part, 16), rows), :]
-    scores[rows * part : rows * part + rows, :] = mm(left, rall[p])
-
-
-def moments_pair(scores, mom, p, between):
+def score_pair(lall, rall, scores, p):
+    scores[p % BUFFERS] = mm(lall[64 * p : 64 * p + 14 * ROWS, :], rall[p])
+
+
+def moments_pair(scores, mom, p):
     shift = iota((ROWS, 128), 0) - (iota((ROWS, 128), 1) & 15)
     valid = (shift >= 0) & (shift <= 12)
     b = (shift - 6).astype(F32)
@@ -163,12 +160,10 @@
         def at(n):
             return scores[ROWS * (n + par) : ROWS * (n + par) + ROWS, cols]
 
-        between(2 * par)
         high = at(0)
         for n in range(1, 13):
             high = jnp.maximum(high, at(n))
         top = jnp.max(jnp.where(valid, high, -3e38), axis=0, keepdims=True)
-        between(2 * par + 1)
         t0 = t1 = t2 = None
         for n in range(12, -1, -1):
             e = jnp.exp2((at(n) - top) * SCALE)
@@ -183,7 +178,14 @@
             mom[p, field : field + 1, cols] = jnp.sum(term, axis=0, keepdims=True)
 
 
-def node_blocks(mom, marks_ref, last, send):
+def node_marks(marks_ref, last, keep):
+    spread = jnp.where((iota((16, 8), 0) >> 1) == iota((16, 8), 1), 1.0, 0.0)
+    marks = mm(spread, marks_ref[...].astype(F32))
+    same = (iota((16, 128), 0) & 1) == (iota((16, 128), 1) >> 6)
+    keep[...] = jnp.where(same, marks, half_turn(marks)) * jnp.where(last, 0.0, 1.0)
+
+
+def node_blocks(mom, keep, send):
     m0, m1, m2, mb, mbb, mab = (mom[:, f, :] for f in range(6))
     r = 1.0 / m0
     n1, mean_b = m1 * r, mb * r
@@ -196,13 +198,14 @@
     p_b = i_ab * mean_a + i_bb * mean_b
     stack = jnp.concatenate([x[:, :128] + x[:, 128:] for x in (i_aa, i_ab, i_bb, p_a, p_b)], axis=0)
     pool = jnp.where((iota((128, 128), 0) >> 1) == (iota((128, 128), 1) & 63), 0.25, 0.0)
-    pooled = jnp.dot(stack, pool, precision=lax.Precision.HIGHEST, preferred_element_type=F32)
-    spread = jnp.where((iota((16, 8), 0) >> 1) == iota((16, 8), 1), 1.0, 0.0)
-    marks = mm(spread, marks_ref[...].astype(F32))
-    same = (iota((16, 128), 0) & 1) == (iota((16, 128), 1) >> 6)
-    marks = jnp.where(same, marks, half_turn(marks)) * jnp.where(last, 0.0, 1.0)
+    high = stack.astype(BF)
+    rest = stack - high.astype(F32)
+    middle = rest.astype(BF)
+    low = (rest - middle.astype(F32)).astype(BF)
+    parts = mm(jnp.concatenate([high, middle, low], axis=0), pool.astype(BF))
+    pooled = parts[:80] + (parts[80:160] + parts[160:])
     for f in range(5):
-        data = pooled[16 * f : 16 * f + 16] * marks
+        data = pooled[16 * f : 16 * f + 16] * keep[...]
         for q in range(16):
             send[q, f : f + 1, :] = data[q : q + 1]
 
@@ -308,6 +311,7 @@
     w1_ref,
     w2_ref,
     marks_ref,
+    keep,
     nwin,
     owin,
     sel,
@@ -319,8 +323,7 @@
     ofm,
     lall,
     rall,
-    scores_a,
-    scores_b,
+    scores,
     mom,
     send_a,
     recv_a,
@@ -374,6 +377,7 @@
     for move in smalls:
         move.wait()
     build_weights(w1_ref, w2_ref, sel, w1b, w2p)
+    node_marks(marks_ref, s == sections - 1, keep)
     nxs[:, 0:16, :] = jnp.zeros((7, 16, 128), BF)
     oxs[:, 0:16, :] = jnp.zeros((7, 16, 128), BF)
     oxs[:, 160:176, :] = jnp.zeros((7, 16, 128), BF)
@@ -400,7 +404,7 @@
     moves += [piece(32 * c, 32 + 32 * c, 2 + c, (before, r)) for c in range(4)]
     moves += [piece(0, 160, 6, (before, up))]
     halo.start()
-    for move in (moves[0], moves[5], *moves[1:5]):
+    for move in moves:
         move.start()
     local.wait()
 
@@ -445,21 +449,14 @@
         for g in range(1, 5) if half == 0 else range(7, 11):
             next_group(nfm, w2p, lall, 32 * r - 6, g)
 
-    score_part(lall, rall, scores_a, 0, 0, 1)
-
-    def two_pairs(i):
-        for now, later, p in ((scores_a, scores_b, 2 * i), (scores_b, scores_a, 2 * i + 1)):
-            q = jnp.minimum(p + 1, 15)
-
-            def ahead(n):
-                if n % (4 // PARTS) == 0:
-                    score_part(lall, rall, later, q, n // (4 // PARTS), PARTS)
-
-            moments_pair(now, mom, p, ahead)
-
-    loop(0, 8, two_pairs)
-
-    node_blocks(mom, marks_ref, s == sections - 1, send_a)
+    for p in range(AHEAD):
+        score_pair(lall, rall, scores, p)
+    for p in range(16):
+        if p + AHEAD < 16:
+            score_pair(lall, rall, scores, p + AHEAD)
+        moments_pair(scores.at[p % BUFFERS], mom, p)
+
+    node_blocks(mom, keep, send_a)
     moves_a = [
         remote(send_a.at[mates[o]  - GROUP * group], recv_a.at[k], asend.at[o - 1], arecv.at[o - 1], (mates[o], r))
         for o in far_first(GROUP)
@@ -522,6 +519,7 @@
             pltpu.VMEM((16, 9), BF),
             pltpu.VMEM((32, 144), BF),
             pltpu.VMEM((8, 128), jnp.int32),
+            pltpu.VMEM((16, 128), F32),
             pltpu.VMEM((192, 512), BF),
             pltpu.VMEM((144, 512), BF),
             pltpu.VMEM((256, 256), BF),
@@ -533,8 +531,7 @@
             pltpu.VMEM((10 * 384, 128), BF),
             pltpu.VMEM((44 * ROWS, 256), BF),
             pltpu.VMEM((16, 256, 256), BF),
-            pltpu.VMEM((14 * ROWS, 256), F32),
-            pltpu.VMEM((14 * ROWS, 256), F32),
+            pltpu.VMEM((BUFFERS, 14 * ROWS, 256), F32),
             pltpu.VMEM((16, 8, 256), F32),
             pltpu.VMEM((GROUP, 5, 128), F32),
             pltpu.VMEM((GROUP, 5, 128), F32),

time: 44.9 us -> 42.3 us (0.942)
  Pallas kernels: 43.4 us -> 40.8 us
    pallas_call x1, Pallas kernels: 43.4 us -> 40.8 us  [body(): pl.pallas_call(lambda *refs: kernel(sections, strips, *refs), out_shape=j...]
where the time goes in v2:
time: 42.3 us; the launch traced here: 42.1 us
  Pallas kernels  40.8 us (96%)
  local copies, waits for them, and re-layouts  1.3 us (3%)
    pallas_call x1, Pallas kernels, body(): pl.pallas_call(lambda *refs: kernel(sections, strips, *refs), out_shape=j...  40.8 us
    unnamed x1, local copies, waits for them, and re-layouts  1.3 us

profile of v2, /device:TPU:1, one launch (start us, length us, event | category | flops | bytes accessed | tf_op | source)
XLA Modules:
  0.0 42.1 jit_solution(15946159496291830958)
XLA Ops:
  0.0 40.8 %shard_map.46 = f32[2,8,128]{2,1,0:T(8,128)} custom-call(bf16[128,512]{1,0:T(8,128)(2,1)} %bitcast.3, bf16[16,9]{1,0:T(8,128)(2,1)} %refs_1_.1, bf16[32,144]{1,0:T(8,128)(2,1)} %refs_2_.1, s32[8,128]{1,0:T(8,128)} %bitcast.5), custom_call_target="tpu_custom_call" | custom-call | tf_op jit(solution)/shard_map/pallas_call | solution.py:513
  40.8 1.3 %copy.7 = f32[2,1,1024]{2,1,0:T(1,128)} copy(f32[2,1,1024]{2,1,0:T(1,128)} %bitcast.4) | data formatting | bytes 16384

commit v3 on v2

--- a/solution.py
+++ b/solution.py
@@ -9,7 +9,7 @@
 MESH = pl.DeviceIdType.MESH
 GROUP = 16
 SPRING, ANCHOR = 8.0, 0.02
-AHEAD, BUFFERS = 3, 4
+AHEAD, BUFFERS = 2, 4
 VMEM_LIMIT = 60 * 1024 * 1024
 ROWS = 32
 SCALE = 32 ** (-0.5) * 1.4426950408889634
@@ -128,6 +128,7 @@
     stack = stack.astype(BF)
     place = jnp.where(iota((144, 128), 0) == iota((144, 128), 1) + 6, 1.0, 0.0).astype(BF)
     ext = lax.dot_general(place, stack, (((1,), (1,)), ((), ())), preferred_element_type=F32)
+    ext = ext.astype(BF)
     rot = [ext] + [pltpu.roll(ext, 32 * k, 1) for k in range(1, 4)]
     lane = iota((32, 128), 1) >> 5
     for q in range(4):
@@ -143,7 +144,7 @@
             )
         lall[128 * g + 32 * q : 128 * g + 32 * q + 32, :] = jnp.concatenate(
             halves, axis=1
-        ).astype(BF)
+        )
 
 
 def score_pair(lall, rall, scores, p):
@@ -379,8 +380,7 @@
     build_weights(w1_ref, w2_ref, sel, w1b, w2p)
     node_marks(marks_ref, s == sections - 1, keep)
     nxs[:, 0:16, :] = jnp.zeros((7, 16, 128), BF)
-    oxs[:, 0:16, :] = jnp.zeros((7, 16, 128), BF)
-    oxs[:, 160:176, :] = jnp.zeros((7, 16, 128), BF)
+    oxs[:, 0:32, :] = jnp.zeros((7, 32, 128), BF)
 
     pl.semaphore_wait(barrier, len(partners))
 
@@ -394,19 +394,19 @@
             device_id_type=MESH,
         )
 
-    halo = remote(image.at[pl.ds(112, 16)], owin.at[pl.ds(0, 16)], isend.at[0], irecv.at[0], (s, down))
+    halo = remote(owin.at[pl.ds(128, 16)], owin.at[pl.ds(0, 16)], isend.at[0], irecv.at[0], (s, down))
     def piece(row, target, n, place):
         return remote(
-            image.at[pl.ds(row, 32)], nwin.at[pl.ds(target, 32)], isend.at[n], irecv.at[n], place
+            owin.at[pl.ds(16 + row, 32)], nwin.at[pl.ds(target, 32)], isend.at[n], irecv.at[n], place
         )
 
     moves = [piece(96, 0, 1, (before, down))]
     moves += [piece(32 * c, 32 + 32 * c, 2 + c, (before, r)) for c in range(4)]
     moves += [piece(0, 160, 6, (before, up))]
+    local.wait()
     halo.start()
     for move in moves:
         move.start()
-    local.wait()
 
     def loop(low, high, step):
         def run(i, carry):
@@ -417,8 +417,8 @@
 
     split_columns(owin, 16, 128, sel, oxs)
     loop(2, 5, lambda i: conv_rows(oxs, w1b, ofm, 3, i))
-    conv_rows(oxs, w1b, ofm, 1, 8)
-    loop(3, 16, lambda i: own_pair(ofm, w2p, rall, i))
+    conv_rows(oxs, w1b, ofm, 7, 1)
+    loop(1, 16, lambda i: own_pair(ofm, w2p, rall, i))
     halo.wait_recv()
 
     @pl.when(r == 0)
@@ -427,34 +427,41 @@
 
     split_columns(owin, 0, 16, sel, oxs)
     conv_rows(oxs, w1b, ofm, 1, 0)
-    for p in range(3):
-        own_pair(ofm, w2p, rall, p)
-
-    for half in range(2):
-        for c in range(3):
-            moves[3 * half + c].wait_recv()
-        edge = 160 * half
-
-        @pl.when(r == (strips - 1) * half)
-        def _():
-            nwin[edge : edge + 32, :] = jnp.zeros((32, 512), BF)
-
-        split_columns(nwin, 96 * half, 96, sel, nxs)
-        block = 6 * half
-        conv_rows(nxs, w1b, nfm, 1, block)
-        conv_rows(nxs, w1b, nfm, 1, block + 2)
-        for g in (0,) if half == 0 else (5, 6):
+    own_pair(ofm, w2p, rall, 0)
+
+    done, group_done, queue, behind = 0, 0, [], []
+    for first, last in ((0, 6),):
+        for c in range(first, last):
+            moves[c].wait_recv()
+            if c in (0, 5):
+
+                @pl.when(r == (0 if c == 0 else strips - 1))
+                def _():
+                    nwin[32 * c : 32 * c + 32, :] = jnp.zeros((32, 512), BF)
+
+        split_columns(nwin, 32 * first, 32 * (last - first), sel, nxs)
+        for g in range(group_done, 2 * last - 1):
+            while done < min(last, (g + 1) // 2 + 1 + 1):
+                conv_rows(nxs, w1b, nfm, 1, 2 * done)
+                done += 1
             next_group(nfm, w2p, lall, 32 * r - 6, g)
-        conv_rows(nxs, w1b, nfm, 1, block + 4)
-        for g in range(1, 5) if half == 0 else range(7, 11):
-            next_group(nfm, w2p, lall, 32 * r - 6, g)
-
-    for p in range(AHEAD):
-        score_pair(lall, rall, scores, p)
-    for p in range(16):
-        if p + AHEAD < 16:
-            score_pair(lall, rall, scores, p + AHEAD)
-        moments_pair(scores.at[p % BUFFERS], mom, p)
+            group_done = g + 1
+            queue += [p for p in range(16) if (2 * p + 13) // 4 == g]
+            while len(queue) > 2:
+                p = queue.pop(0)
+                score_pair(lall, rall, scores, p)
+                behind.append(p)
+                if len(behind) > AHEAD:
+                    p = behind.pop(0)
+                    moments_pair(scores.at[p % BUFFERS], mom, p)
+    while behind or queue:
+        if behind:
+            p = behind.pop(0)
+            moments_pair(scores.at[p % BUFFERS], mom, p)
+        if queue:
+            p = queue.pop(0)
+            score_pair(lall, rall, scores, p)
+            behind.append(p)
 
     node_blocks(mom, keep, send_a)
     moves_a = [

time: 42.3 us -> 41.4 us (0.979)
  Pallas kernels: 40.8 us -> 39.9 us
    pallas_call x1, Pallas kernels: 40.8 us -> 39.9 us  [body(): pl.pallas_call(lambda *refs: kernel(sections, strips, *refs), out_shape=j...]
where the time goes in v3:
time: 41.4 us; the launch traced here: 41.2 us
  Pallas kernels  39.9 us (96%)
  local copies, waits for them, and re-layouts  1.3 us (3%)
    pallas_call x1, Pallas kernels, body(): pl.pallas_call(lambda *refs: kernel(sections, strips, *refs), out_shape=j...  39.9 us
    unnamed x1, local copies, waits for them, and re-layouts  1.3 us

profile of v3, /device:TPU:1, one launch (start us, length us, event | category | flops | bytes accessed | tf_op | source)
XLA Modules:
  0.0 41.2 jit_solution(10468932637266021158)
XLA Ops:
  0.0 39.9 %shard_map.46 = f32[2,8,128]{2,1,0:T(8,128)} custom-call(bf16[128,512]{1,0:T(8,128)(2,1)} %bitcast.3, bf16[16,9]{1,0:T(8,128)(2,1)} %refs_1_.1, bf16[32,144]{1,0:T(8,128)(2,1)} %refs_2_.1, s32[8,128]{1,0:T(8,128)} %bitcast.5), custom_call_target="tpu_custom_call" | custom-call | tf_op jit(solution)/shard_map/pallas_call | solution.py:520
  39.9 1.3 %copy.7 = f32[2,1,1024]{2,1,0:T(1,128)} copy(f32[2,1,1024]{2,1,0:T(1,128)} %bitcast.4) | data formatting | bytes 16384

commit v4 on v3

--- a/solution.py
+++ b/solution.py
@@ -206,9 +206,7 @@
     parts = mm(jnp.concatenate([high, middle, low], axis=0), pool.astype(BF))
     pooled = parts[:80] + (parts[80:160] + parts[160:])
     for f in range(5):
-        data = pooled[16 * f : 16 * f + 16] * keep[...]
-        for q in range(16):
-            send[q, f : f + 1, :] = data[q : q + 1]
+        send[:, f, :] = pooled[16 * f : 16 * f + 16] * keep[...]
 
 
 def segment(recv, group, sections, low, high):
@@ -447,7 +445,7 @@
             next_group(nfm, w2p, lall, 32 * r - 6, g)
             group_done = g + 1
             queue += [p for p in range(16) if (2 * p + 13) // 4 == g]
-            while len(queue) > 2:
+            while len(queue) > 4:
                 p = queue.pop(0)
                 score_pair(lall, rall, scores, p)
                 behind.append(p)
@@ -471,6 +469,8 @@
     for move in moves_a:
         move.start()
     recv_a[k] = send_a[k]
+    for move in (halo, *moves):
+        move.wait_send()
     for move in moves_a:
         move.wait_recv()
 
@@ -484,6 +484,8 @@
     for move in moves_b:
         move.start()
     recv_b[group] = send_b[...]
+    for move in moves_a:
+        move.wait_send()
     for move in moves_b:
         move.wait_recv()
 
@@ -492,25 +494,28 @@
     left8 = iota((8, 128), 1) < 64
     front = jnp.where(left8, xa, half_turn(xb))
     rear = jnp.where(left8, half_turn(xa), xb)
-    for j in range(8):
-        send_c[j] = front[j : j + 1]
-        send_c[GROUP - 1 - j] = rear[j : j + 1]
+    send_c[0:8, 0, :] = front
+    send_c[8:16, 0, :] = rear
+
+    def place_of(m):
+        return m + lax.div(m, 8) * (23 - 2 * m)
+
     slot = 8 * lax.rem(k, 2) + lax.div(k, 2)
     moves_c = [
-        remote(send_c.at[mates[o] - GROUP * group], recv_c.at[slot], csend.at[o - 1], crecv.at[o - 1], (mates[o], r))
+        remote(send_c.at[place_of(mates[o] - GROUP * group)], recv_c.at[slot], csend.at[o - 1], crecv.at[o - 1], (mates[o], r))
         for o in far_first(GROUP)
     ]
     for move in moves_c:
         move.start()
-    recv_c[slot] = send_c[k]
+    recv_c[slot] = send_c[place_of(k)]
+    for move in moves_b + moves_c:
+        move.wait_send()
     for move in moves_c:
         move.wait_recv()
-    even = jnp.concatenate([recv_c[q] for q in range(8)], axis=0)
-    odd = jnp.concatenate([recv_c[q] for q in range(8, 16)], axis=0)
+    even = recv_c[0:8, 0, :]
+    odd = recv_c[8:16, 0, :]
     out_ref[0] = jnp.where(left8, even, half_turn(odd))
     out_ref[1] = jnp.where(left8, half_turn(even), odd)
-    for move in (halo, *moves, *moves_a, *moves_b, *moves_c):
-        move.wait_send()
 
 
 def body(sections, strips, image, conv_one, conv_two, tissue):

time: 41.4 us -> 41.3 us (level)
  no operation moved by 1% of the time
where the time goes in v4:
time: 41.3 us; the launch traced here: 41.1 us
  Pallas kernels  39.8 us (96%)
  local copies, waits for them, and re-layouts  1.3 us (3%)
    pallas_call x1, Pallas kernels, body(): pl.pallas_call(lambda *refs: kernel(sections, strips, *refs), out_shape=j...  39.8 us
    unnamed x1, local copies, waits for them, and re-layouts  1.3 us

profile of v4, /device:TPU:1, one launch (start us, length us, event | category | flops | bytes accessed | tf_op | source)
XLA Modules:
  0.0 41.1 jit_solution(4343992331271847911)
XLA Ops:
  0.0 39.8 %shard_map.46 = f32[2,8,128]{2,1,0:T(8,128)} custom-call(bf16[128,512]{1,0:T(8,128)(2,1)} %bitcast.3, bf16[16,9]{1,0:T(8,128)(2,1)} %refs_1_.1, bf16[32,144]{1,0:T(8,128)(2,1)} %refs_2_.1, s32[8,128]{1,0:T(8,128)} %bitcast.5), custom_call_target="tpu_custom_call" | custom-call | tf_op jit(solution)/shard_map/pallas_call | solution.py:525
  39.8 1.3 %copy.7 = f32[2,1,1024]{2,1,0:T(1,128)} copy(f32[2,1,1024]{2,1,0:T(1,128)} %bitcast.4) | data formatting | bytes 16384

commit v5 on v4

--- a/solution.py
+++ b/solution.py
@@ -439,7 +439,7 @@
 
         split_columns(nwin, 32 * first, 32 * (last - first), sel, nxs)
         for g in range(group_done, 2 * last - 1):
-            while done < min(last, (g + 1) // 2 + 1 + 1):
+            while done < min(last, (g + 1) // 2 + 1 + 2):
                 conv_rows(nxs, w1b, nfm, 1, 2 * done)
                 done += 1
             next_group(nfm, w2p, lall, 32 * r - 6, g)

time: 41.3 us -> 41.4 us (level)
  no operation moved by 1% of the time
where the time goes in v5:
time: 41.4 us; the launch traced here: 41.2 us
  Pallas kernels  39.9 us (96%)
  local copies, waits for them, and re-layouts  1.3 us (3%)
    pallas_call x1, Pallas kernels, body(): pl.pallas_call(lambda *refs: kernel(sections, strips, *refs), out_shape=j...  39.9 us
    unnamed x1, local copies, waits for them, and re-layouts  1.3 us

profile of v5, /device:TPU:1, one launch (start us, length us, event | category | flops | bytes accessed | tf_op | source)
XLA Modules:
  0.0 41.2 jit_solution(18056913506807322921)
XLA Ops:
  0.0 39.9 %shard_map.46 = f32[2,8,128]{2,1,0:T(8,128)} custom-call(bf16[128,512]{1,0:T(8,128)(2,1)} %bitcast.3, bf16[16,9]{1,0:T(8,128)(2,1)} %refs_1_.1, bf16[32,144]{1,0:T(8,128)(2,1)} %refs_2_.1, s32[8,128]{1,0:T(8,128)} %bitcast.5), custom_call_target="tpu_custom_call" | custom-call | tf_op jit(solution)/shard_map/pallas_call | solution.py:525
  39.9 1.3 %copy.7 = f32[2,1,1024]{2,1,0:T(1,128)} copy(f32[2,1,1024]{2,1,0:T(1,128)} %bitcast.4) | data formatting | bytes 16384
